TPU v7x, 32 devices: a whole 2x2x4 slice. The times are simulated.
32 devices in a mesh: atom: 16 (over z, y, core), aux: 2 (over x).
Axes of the slice: x: 2, y: 2, z: 4, core: 2. Of those that a mesh axis runs over, the one named last changes fastest.
Arguments:
- three: bfloat16 [32, 128, 128, 384], P('atom', 'aux'), may hold values from -0.5 to 0.5
- occupied: bfloat16 [4096, 384], P(('atom', 'aux')), may hold values from -0.3125 to 0.3125
- virtual: bfloat16 [4096, 384], P(('atom', 'aux')), may hold values from -0.3125 to 0.3125
- three_mask: int32 [32, 3], replicated, may hold values from 0 to 1, as said below
- occ_mask: int32 [32, 3], replicated, may hold values from 0 to 1, as said below
- vir_mask: int32 [32, 3], replicated, may hold values from 0 to 1, as said below
- atom_sizes: int32 [32], replicated, may hold values from 64 to 128
Outputs:
- polarizability: float32 [32, 128, 384], P('atom', 'aux')
Inputs may be any that keep to these rules, and one draw needn't show every extreme that they name: three_mask[b, 1] = 1 for every block b; the slab pairs its atom blocks into molecules of two, and every block keeps its tile towards the neighbouring molecule: three_mask[b, 0] = 1 for even b and three_mask[b, 2] = 1 for odd b. occ_mask[b, 1] = 1 for every block b; occ_mask[b, 0] = 1 where b is a multiple of 2, and occ_mask[b, 2] = 1 where b + 1 is a multiple of 2. vir_mask[b, 1] = 1 for every block b.
All inputs are finite; a program needn't handle non-finite values.
Results may differ from a plain program's by a relative error of at most 0.0041.
Values may be sent and summed in bfloat16 or wider, within the bound.
A program may use at most 320 MiB of HBM per device.

v0:
```python
import jax
import jax.numpy as jnp
from jax import lax
from jax.sharding import PartitionSpec as P


def with_halo(cells, sides, width):
    for axis, dim in sides:
        count = lax.axis_size(axis)
        head = lax.slice_in_dim(cells, 0, width, axis=dim)
        tail = lax.slice_in_dim(cells, cells.shape[dim] - width, cells.shape[dim], axis=dim)
        cells = jnp.concatenate(
            [
                lax.ppermute(tail, axis, [(i, (i + 1) % count) for i in range(count)]),
                cells,
                lax.ppermute(head, axis, [((i + 1) % count, i) for i in range(count)]),
            ],
            axis=dim,
        )
    return cells


def from_behind(value, axis, steps):
    count = lax.axis_size(axis)
    pairs = [(source, (source + steps) % count) for source in range(count)]
    return lax.ppermute(value, axis, pairs)


def pick_sizes(lookup, blocks):
    matches = blocks[:, None] == jnp.arange(lookup.shape[0], dtype=jnp.int32)[None, :]
    return jnp.sum(jnp.where(matches, lookup[None, :], 0), axis=1)


def pick_rows(lookup, blocks):
    matches = blocks[:, None] == jnp.arange(lookup.shape[0], dtype=jnp.int32)[None, :]
    return jnp.sum(jnp.where(matches[:, :, None], lookup[None, :, :], 0), axis=1)


def block_ids(first_block, block_count, total_blocks):
    return (first_block + jnp.arange(block_count, dtype=jnp.int32) + total_blocks) % total_blocks


def band_live(atom_sizes, mask_table, blocks, block_width):
    total_blocks = atom_sizes.shape[0]
    block_count = blocks.shape[0]
    inside = jnp.arange(block_width, dtype=jnp.int32)
    partners = (
        blocks[:, None] + jnp.arange(3, dtype=jnp.int32)[None, :] + total_blocks - 1
    ) % total_blocks
    own_size = pick_sizes(atom_sizes, blocks)
    partner_size = pick_sizes(atom_sizes, partners.reshape(-1)).reshape(block_count, 3)
    live_blocks = pick_rows(mask_table, blocks) > 0
    row_ok = inside[None, :] < own_size[:, None]
    col_ok = inside[None, None, :] < partner_size[:, :, None]
    both = row_ok[:, :, None, None] & col_ok[:, None, :, :] & live_blocks[:, None, :, None]
    return both.reshape(block_count, block_width, 3 * block_width)


def block_live(mask_table, blocks, block_width):
    block_count = blocks.shape[0]
    live_blocks = pick_rows(mask_table, blocks) > 0
    spread = jnp.broadcast_to(
        live_blocks[:, None, :, None], (block_count, block_width, 3, block_width)
    )
    return spread.reshape(block_count * block_width, 3 * block_width)


def shards(three, occupied, virtual, three_mask, occ_mask, vir_mask, atom_sizes):
    zero_bf = jnp.zeros((), jnp.bfloat16)
    block_count = three.shape[0]
    aux_local = three.shape[1]
    block_width = three.shape[2]
    total_blocks = atom_sizes.shape[0]
    first_block = lax.axis_index("atom") * block_count
    local_ids = block_ids(first_block, block_count, total_blocks)
    band_ok = band_live(atom_sizes, three_mask, local_ids, block_width)
    coupling = jnp.where(band_ok[:, None], three, zero_bf)
    occ_rows, vir_rows = (
        lax.all_gather(occupied, "aux", axis=0, tiled=True),
        lax.all_gather(virtual, "aux", axis=0, tiled=True),
    )
    occ_live = jnp.where(block_live(occ_mask, local_ids, block_width), occ_rows, zero_bf)
    vir_live = jnp.where(block_live(vir_mask, local_ids, block_width), vir_rows, zero_bf)
    vir_ext = with_halo(vir_live, (("atom", 0),), block_width)
    mixed = None
    for offset in range(3):
        coupled = coupling[:, :, :, offset * block_width : (offset + 1) * block_width]
        partner_rows = vir_ext[offset * block_width : (offset + block_count) * block_width]
        partner_rows = partner_rows.reshape(block_count, block_width, 3 * block_width)
        product = jnp.einsum(
            "lpmb,lbc->lpmc", coupled, partner_rows, preferred_element_type=jnp.float32
        )
        padded = jnp.pad(
            product, ((0, 0), (0, 0), (0, 0), (offset * block_width, (2 - offset) * block_width))
        )
        mixed = padded if offset == 0 else mixed + padded
    mixed = mixed.astype(jnp.bfloat16)
    occ_tiles = occ_live.reshape(block_count, block_width, 3 * block_width)
    paired = []
    for target in range(3):
        density = occ_tiles[:, :, target * block_width : (target + 1) * block_width]
        screened = jnp.einsum(
            "lmj,lpmc->lpjc",
            density,
            mixed[:, :, :, target * block_width : (target + 3) * block_width],
            preferred_element_type=jnp.float32,
        )
        paired.append(screened.astype(jnp.bfloat16))
    from_left = from_behind(paired[2][-1], "atom", 1)
    from_right = from_behind(paired[0][0], "atom", -1)
    before = jnp.concatenate([from_left[None], paired[2][:-1]], axis=0)
    after = jnp.concatenate([paired[0][1:], from_right[None]], axis=0)
    sources = jnp.stack([before, paired[1], after], axis=1)
    total_aux = aux_local * lax.axis_size("aux")
    tile_sum = jnp.einsum(
        "lqrc,loprc->lqop",
        lax.all_gather(coupling, "aux", axis=1, tiled=True),
        sources,
        preferred_element_type=jnp.float32,
    )
    swapped = lax.all_to_all(tile_sum, "aux", split_axis=1, concat_axis=3, tiled=True)
    return swapped.reshape(block_count, aux_local, 3 * total_aux)


def solution(mesh):
    in_specs = (
        P("atom", "aux", None, None),
        P(("atom", "aux"), None),
        P(("atom", "aux"), None),
        P(),
        P(),
        P(),
        P(),
    )
    out_specs = P("atom", "aux", None)
    return jax.shard_map(shards, mesh=mesh, in_specs=in_specs, out_specs=out_specs, check_vma=False)
```

profile of v0, /device:TPU:0, one launch (start us, length us, event | category | flops | bytes accessed | tf_op | source)
XLA Modules:
  0.0 395.9 jit_solution(6158620312043457783)
XLA Ops:
  6.7 1.0 select_reduce_fusion.1
  8.0 0.8 select_reduce_fusion.4
  8.8 0.8 select_reduce_fusion
  10.0 10.5 %broadcast_select_fusion = bf16[2,64,128,384]{3,2,1,0:T(8,128)(2,1)} fusion(bf16[2,64,128,384]{3,2,1,0:T(8,128)(2,1)} %param.7, pred[2,128,384]{2,1,0:T(8,128)(4,1)S(1)} %and_and_fusion), kind=kLoop, calls=%fused_computation.15 | loop fusion | flops 6291456 | bytes 25264128 | tf_op jit(solution)/shard_map/jit(_where)/select_n | solution.py:77
  20.7 0.7 copy-done.1
  21.5 6.4 %all_gather.10 = bf16[256,384]{1,0:T(8,128)(2,1)S(1)} all-gather(bf16[128,384]{1,0:T(8,128)(2,1)S(1)} %copy-done.1), channel_id=1, replica_groups=mesh['atom'=16,'aux'=2] {'aux'}, dimensions={0}, use_global_device_ids=true | all-gather | bytes 294912 | tf_op jit(solution)/shard_map/all_gather | solution.py:80
  28.2 4.4 %collective-permute-start.1 = (bf16[128,384]{1,0:T(8,128)(2,1)S(1)}, bf16[128,384]{1,0:T(8,128)(2,1)S(1)}, u32[]{:S(2)}, u32[]{:S(2)}) collective-permute-start(bf16[128,384]{1,0:T(8,128)(2,1)S(1)} %get-tuple-element.15), channel_id=1, source_target_pairs={{2,0},{4,2},{6,4},{8,6},{10,8},{12,10},{14,12},{16,14},{18,16},{20... | collective-permute-start | bytes 294920 | tf_op jit(solution)/shard_map/ppermute | solution.py:16
  32.7 5.3 %all_gather.11 = bf16[256,384]{1,0:T(8,128)(2,1)S(1)} all-gather(bf16[128,384]{1,0:T(8,128)(2,1)S(1)} %copy-done.2), channel_id=1, replica_groups=mesh['atom'=16,'aux'=2] {'aux'}, dimensions={0}, use_global_device_ids=true | all-gather | bytes 294912 | tf_op jit(solution)/shard_map/all_gather | solution.py:79
  38.0 18.0 %fusion.16 = f32[2,64,128,384]{3,2,1,0:T(8,128)} fusion(bf16[2,128,384,1]{2,1,3,0:T(8,128)(2,1)S(1)} %bitcast.82, bf16[2,64,128,384]{3,2,1,0:T(8,128)(2,1)} %broadcast_select_fusion), kind=kOutput, calls=%fused_computation.20 | convolution fusion | flops 1610612736 | bytes 29556736 | tf_op jit(solution)/shard_map/lpmb,lbc->lpmc/dot_general | solution.py:90
  56.2 14.6 %fusion.14 = f32[2,64,128,384]{3,2,1,0:T(8,128)} fusion(bf16[2,128,384,1]{2,1,3,0:T(8,128)(2,1)S(1)} %bitcast.89, bf16[2,64,128,384]{3,2,1,0:T(8,128)(2,1)} %broadcast_select_fusion), kind=kOutput, calls=%fused_computation.18 | convolution fusion | flops 1610612736 | bytes 29556736 | tf_op jit(solution)/shard_map/lpmb,lbc->lpmc/dot_general | solution.py:90
  70.8 13.9 %fusion.18 = f32[2,64,128,384]{3,2,1,0:T(8,128)} fusion(bf16[2,128,384,1]{2,1,3,0:T(8,128)(2,1)S(1)} %bitcast.88, bf16[2,64,128,384]{3,2,1,0:T(8,128)(2,1)} %broadcast_select_fusion), kind=kOutput, calls=%fused_computation.22 | convolution fusion | flops 1610612736 | bytes 29556736 | tf_op jit(solution)/shard_map/lpmb,lbc->lpmc/dot_general | solution.py:90
  84.7 31.3 %add_convert_fusion = bf16[2,64,128,640]{3,2,1,0:T(8,128)(2,1)} fusion(f32[2,64,128,384]{3,2,1,0:T(8,128)} %fusion.14, f32[2,64,128,384]{3,2,1,0:T(8,128)} %fusion.16, f32[2,64,128,384]{3,2,1,0:T(8,128)} %fusion.18), kind=kLoop, calls=%fused_computation | loop fusion | flops 31457280 | bytes 96468992 | tf_op jit(solution)/shard_map/convert_element_type | solution.py:97
  116.0 10.5 %convert_bitcast_fusion.2 = bf16[2,64,128,384]{2,3,1,0:T(8,128)(2,1)} fusion(bf16[2,64,128,640]{3,2,1,0:T(8,128)(2,1)} %add_convert_fusion, bf16[2,128,384]{2,1,0:T(8,128)(2,1)S(1)} %bitcast.85), kind=kOutput, calls=%fused_computation.14 | convolution fusion | flops 1616904192 | bytes 25231360 | tf_op jit(solution)/shard_map/lmj,lpmc->lpjc/dot_general | solution.py:102
  126.5 9.7 %slice_bitcast_fusion.1 = (bf16[64,128,384]{1,2,0:T(8,128)(2,1)}, bf16[1,64,128,384]{2,3,1,0:T(8,128)(2,1)S(1)}) fusion(bf16[2,64,128,384]{2,3,1,0:T(8,128)(2,1)} %convert_bitcast_fusion.2), kind=kLoop, calls=%fused_computation.17 | loop fusion | bytes 25165824 | tf_op jit(solution)/shard_map/squeeze | solution.py:109
  136.2 10.5 %convert_bitcast_fusion = bf16[2,64,128,384]{2,3,1,0:T(8,128)(2,1)} fusion(bf16[2,64,128,640]{3,2,1,0:T(8,128)(2,1)} %add_convert_fusion, bf16[2,128,384]{2,1,0:T(8,128)(2,1)S(1)} %bitcast.86), kind=kOutput, calls=%fused_computation.12 | convolution fusion | flops 1616904192 | bytes 25231360 | tf_op jit(solution)/shard_map/lmj,lpmc->lpjc/dot_general | solution.py:102
  146.8 12.5 %fusion.25 = (bf16[1,64,128,384]{2,3,1,0:T(8,128)(2,1)}, bf16[64,128,384]{1,2,0:T(8,128)(2,1)}) fusion(bf16[2,64,128,384]{2,3,1,0:T(8,128)(2,1)} %convert_bitcast_fusion), kind=kLoop, calls=%fused_computation.58 | loop fusion | bytes 25165824 | tf_op jit(solution)/shard_map/slice | solution.py:112
  159.2 4.4 %collective-permute-start.3 = (bf16[64,128,384]{1,2,0:T(8,128)(2,1)}, bf16[64,128,384]{1,2,0:T(8,128)(2,1)}, u32[]{:S(2)}, u32[]{:S(2)}) collective-permute-start(bf16[64,128,384]{1,2,0:T(8,128)(2,1)} %get-tuple-element.11), channel_id=1, source_target_pairs={{0,30},{2,0},{4,2},{6,4},{8,6},{10,8},{12,10},{14,12},{16,14},{18,... | collective-permute-start | bytes 18874376 | tf_op jit(solution)/shard_map/ppermute | solution.py:26
  163.7 10.5 %convert_bitcast_fusion.1 = bf16[2,1,64,128,384]{3,4,2,0,1:T(8,128)(2,1)} fusion(bf16[2,64,128,640]{3,2,1,0:T(8,128)(2,1)} %add_convert_fusion, bf16[2,128,384]{2,1,0:T(8,128)(2,1)S(1)} %bitcast.87), kind=kOutput, calls=%fused_computation.13 | convolution fusion | flops 1616904192 | bytes 25231360 | tf_op jit(solution)/shard_map/lmj,lpmc->lpjc/dot_general | solution.py:102
  174.2 35.5 %collective-permute-done.2 = bf16[64,128,384]{1,2,0:T(8,128)(2,1)} collective-permute-done((bf16[64,128,384]{1,2,0:T(8,128)(2,1)}, bf16[64,128,384]{1,2,0:T(8,128)(2,1)}, u32[]{:S(2)}, u32[]{:S(2)}) %collective-permute-start.2) | collective-permute-done | bytes 6291488 | tf_op jit(solution)/shard_map/ppermute | solution.py:26
  209.7 9.2 %maximum_bitcast_fusion = bf16[2,1,64,128,384]{3,4,2,0,1:T(8,128)(2,1)} fusion(bf16[1,64,128,384]{2,3,1,0:T(8,128)(2,1)S(1)} %get-tuple-element.9, bf16[1,64,128,384]{2,3,1,0:T(8,128)(2,1)} %bitcast.16), kind=kLoop, calls=%fused_computation.10 | loop fusion | flops 6291456 | bytes 25165824 | tf_op jit(solution)/shard_map/stack | solution.py:113
  218.9 13.5 %collective-permute-done.3 = bf16[64,128,384]{1,2,0:T(8,128)(2,1)} collective-permute-done((bf16[64,128,384]{1,2,0:T(8,128)(2,1)}, bf16[64,128,384]{1,2,0:T(8,128)(2,1)}, u32[]{:S(2)}, u32[]{:S(2)}) %collective-permute-start.3) | collective-permute-done | bytes 6291488 | tf_op jit(solution)/shard_map/ppermute | solution.py:26
  232.5 8.3 %maximum_bitcast_fusion.1 = bf16[2,1,64,128,384]{3,4,2,0,1:T(8,128)(2,1)} fusion(bf16[1,64,128,384]{2,3,1,0:T(8,128)(2,1)} %bitcast.26, bf16[1,64,128,384]{2,3,1,0:T(8,128)(2,1)S(1)} %copy-done), kind=kLoop, calls=%fused_computation.11 | loop fusion | flops 6291456 | bytes 25165824 | tf_op jit(solution)/shard_map/stack | solution.py:113
  240.8 25.7 %pad_maximum_fusion = bf16[2,3,64,128,384]{3,4,2,0,1:T(8,128)(2,1)} fusion(bf16[2,1,64,128,384]{3,4,2,0,1:T(8,128)(2,1)} %maximum_bitcast_fusion.1, bf16[2,1,64,128,384]{3,4,2,0,1:T(8,128)(2,1)} %convert_bitcast_fusion.1, bf16[2,1,64,128,384]{3,4,2,0,1:T(8,128)(2,1)} %maximum_bitcast_fusion), kind=kLoop, calls=%fused_computation.1 | loop fusion | flops 37748736 | bytes 75497472 | tf_op jit(solution)/shard_map/stack | solution.py:113
  266.5 51.7 %all-gather.2.cloned.1.call-done = bf16[2,128,128,384]{3,2,1,0:T(8,128)(2,1)} async-done(((bf16[2,64,128,384]{3,2,1,0:T(8,128)(2,1)}), bf16[2,128,128,384]{3,2,1,0:T(8,128)(2,1)}) %all-gather.2.cloned.1.call-update) | async-done | bytes 25165840 | tf_op jit(solution)/shard_map/all_gather | solution.py:117
  318.2 32.1 %copy.65 = bf16[2,128,128,384,1]{2,1,3,4,0:T(8,128)(2,1)} copy(bf16[2,128,128,384,1]{3,2,1,0,4:T(8,128)(2,1)} %bitcast.81) | data formatting | bytes 50331648 | tf_op jit(solution)/shard_map/all_gather | solution.py:117
  350.3 27.3 %fusion.20 = f32[2,128,3,64]{1,3,2,0:T(8,128)S(1)} fusion(bf16[2,128,128,384,1]{2,1,3,4,0:T(8,128)(2,1)} %copy.65, bf16[2,3,64,128,384]{3,4,2,0,1:T(8,128)(2,1)} %pad_maximum_fusion), kind=kOutput, calls=%fused_computation.24 | convolution fusion | flops 4831838208 | bytes 63111168 | tf_op jit(solution)/shard_map/lqrc,loprc->lqop/dot_general | solution.py:115
  378.0 0.4 reshape.145
  378.4 7.2 %all_to_all.15 = f32[2,1,24576]{2,1,0:T(1,128)S(1)} all-to-all(f32[2,1,24576]{2,1,0:T(1,128)S(1)} %reshape.145), channel_id=1, replica_groups=mesh['atom'=16,'aux'=2] {'aux'}, dimensions={0} | all-to-all | bytes 393216 | tf_op jit(solution)/shard_map/all_to_all | solution.py:121
  385.6 0.5 broadcast.157
  386.1 1.2 reduce
  387.3 0.4 reshape.146
  388.0 1.0 reshape.136
  (37 shorter events, 2.2 us)
Async XLA Ops:
  6.5 311.7 %all-gather.2.cloned.1.call-start = ((), (), s32[]{:S(2)}) async-start(), calls=%async_computation.1 | async-start | bytes 37748736 | tf_op jit(solution)/shard_map/all_gather | solution.py:117
  20.6 0.9 copy-start.1
  20.6 12.1 %copy-start.2 = (bf16[128,384]{1,0:T(8,128)(2,1)S(1)}, bf16[128,384]{1,0:T(8,128)(2,1)}, u32[]{:S(2)}) copy-start(bf16[128,384]{1,0:T(8,128)(2,1)} %param.8) | copy-start | bytes 294916
  28.1 28.1 %collective-permute-start = (bf16[128,384]{1,0:T(8,128)(2,1)S(1)}, bf16[128,384]{1,0:T(8,128)(2,1)S(1)}, u32[]{:S(2)}, u32[]{:S(2)}) collective-permute-start(bf16[128,384]{1,0:T(8,128)(2,1)S(1)} %get-tuple-element.14), channel_id=1, source_target_pairs={{0,2},{2,4},{4,6},{6,8},{8,10},{10,12},{12,14},{14,16},{16,18},{18... | collective-permute-start | bytes 294920 | tf_op jit(solution)/shard_map/ppermute | solution.py:14
  28.2 28.0 %collective-permute-start.1 = (bf16[128,384]{1,0:T(8,128)(2,1)S(1)}, bf16[128,384]{1,0:T(8,128)(2,1)S(1)}, u32[]{:S(2)}, u32[]{:S(2)}) collective-permute-start(bf16[128,384]{1,0:T(8,128)(2,1)S(1)} %get-tuple-element.15), channel_id=1, source_target_pairs={{2,0},{4,2},{6,4},{8,6},{10,8},{12,10},{14,12},{16,14},{18,16},{20... | collective-permute-start | bytes 294920 | tf_op jit(solution)/shard_map/ppermute | solution.py:16
  136.2 73.5 %collective-permute-start.2 = (bf16[64,128,384]{1,2,0:T(8,128)(2,1)}, bf16[64,128,384]{1,2,0:T(8,128)(2,1)}, u32[]{:S(2)}, u32[]{:S(2)}) collective-permute-start(bf16[64,128,384]{1,2,0:T(8,128)(2,1)} %get-tuple-element.8), channel_id=1, source_target_pairs={{0,2},{2,4},{4,6},{6,8},{8,10},{10,12},{12,14},{14,16},{16,18},{18... | collective-permute-start | bytes 18874376 | tf_op jit(solution)/shard_map/ppermute | solution.py:26
  159.2 73.2 %collective-permute-start.3 = (bf16[64,128,384]{1,2,0:T(8,128)(2,1)}, bf16[64,128,384]{1,2,0:T(8,128)(2,1)}, u32[]{:S(2)}, u32[]{:S(2)}) collective-permute-start(bf16[64,128,384]{1,2,0:T(8,128)(2,1)} %get-tuple-element.11), channel_id=1, source_target_pairs={{0,30},{2,0},{4,2},{6,4},{8,6},{10,8},{12,10},{14,12},{16,14},{18,... | collective-permute-start | bytes 18874376 | tf_op jit(solution)/shard_map/ppermute | solution.py:26
  209.7 22.8 %copy-start = (bf16[1,64,128,384]{2,3,1,0:T(8,128)(2,1)S(1)}, bf16[1,64,128,384]{2,3,1,0:T(8,128)(2,1)}, u32[]{:S(2)}) copy-start(bf16[1,64,128,384]{2,3,1,0:T(8,128)(2,1)} %get-tuple-element.10) | copy-start | bytes 18874372
Sparse Core Ops, SparseCore 0:
  20.7 297.4 all-gather.1
where the time goes:
time: 397 us; the launch traced here: 396 us
  matrix products  105 us (26%)
  waiting for transfers between devices  101 us (25%)
  other arithmetic  89.5 us (23%)
  local copies, waits for them, and re-layouts  58.8 us (15%)
  blocking collectives  18.9 us (5%)
  between operations  13.5 us (3%)
  starting transfers between devices  8.93 us (2%)
    all_gather x1, waiting for transfers between devices, shards(): lax.all_gather(coupling, 'aux', axis=1, tiled=True)  51.7 us
    ppermute x2, waiting for transfers between devices, from_behind(): return lax.ppermute(value, axis, pairs)  49 us
    dot_general x3, matrix products, shards(): jnp.einsum('lpmb,lbc->lpmc', coupled, partner_rows, preferred_element_typ...  46.5 us
    another operation x3, other arithmetic, shards(): sources = jnp.stack([before, paired[1], after], axis=1)  43.2 us
    all_gather x1, local copies, waits for them, and re-layouts, shards(): lax.all_gather(coupling, 'aux', axis=1, tiled=True)  32.1 us
    dot_general x3, matrix products, shards(): jnp.einsum('lmj,lpmc->lpjc', density, mixed[:, :, :, target * block_width...  31.6 us
    convert_element_type x1, other arithmetic, shards(): mixed = mixed.astype(jnp.bfloat16)  31.3 us
    dot_general x1, matrix products, shards(): jnp.einsum('lqrc,loprc->lqop', lax.all_gather(coupling, 'aux', axis=1, ti...  27.3 us
  transfers between devices with their start and end apart: 5, of which 3 were waited for; matrix products, arithmetic and copies ran while one was open for 44% of the time, Pallas kernels for 0%

commit v1 on v0

--- a/solution.py
+++ b/solution.py
@@ -2,6 +2,18 @@
 import jax.numpy as jnp
 from jax import lax
 from jax.sharding import PartitionSpec as P
+
+
+def doubled_up(x, axis, dim):
+    ways, here = (lax.axis_size(axis), lax.axis_index(axis))
+    grown, reach = (x, 1)
+    while reach < ways:
+        theirs = lax.ppermute(grown, axis, [(d, d ^ reach) for d in range(ways)])
+        mine_first = jnp.concatenate([grown, theirs], axis=dim)
+        theirs_first = jnp.concatenate([theirs, grown], axis=dim)
+        grown = jnp.where(here & reach == 0, mine_first, theirs_first)
+        reach = 2 * reach
+    return grown
 
 
 def with_halo(cells, sides, width):
@@ -114,7 +126,7 @@
     total_aux = aux_local * lax.axis_size("aux")
     tile_sum = jnp.einsum(
         "lqrc,loprc->lqop",
-        lax.all_gather(coupling, "aux", axis=1, tiled=True),
+        doubled_up(coupling, "aux", 1),
         sources,
         preferred_element_type=jnp.float32,
     )

time: 397 us -> 657 us (1.65)
  the two profiles are of different devices: /device:TPU:0 before, /device:TPU:20 now
where the time goes in v1:
time: 657 us; the launch traced here: 656 us
  blocking collectives  272 us (41%)
  other arithmetic  114 us (17%)
  waiting for transfers between devices  102 us (16%)
  matrix products  101 us (15%)
  local copies, waits for them, and re-layouts  61.3 us (9%)
    all_gather x1, blocking collectives, shards(): lax.all_gather(occupied, 'aux', axis=0, tiled=True)  259 us
    ppermute x2, waiting for transfers between devices, from_behind(): return lax.ppermute(value, axis, pairs)  102 us
    another operation x3, other arithmetic, shards(): sources = jnp.stack([before, paired[1], after], axis=1)  43.2 us
    dot_general x3, matrix products, shards(): jnp.einsum('lpmb,lbc->lpmc', coupled, partner_rows, preferred_element_typ...  41.8 us
    select_n x1, local copies, waits for them, and re-layouts, doubled_up(): grown = jnp.where(here & reach == 0, mine_first, theirs_first)  32.2 us
    dot_general x3, matrix products, shards(): jnp.einsum('lmj,lpmc->lpjc', density, mixed[:, :, :, target * block_width...  31.9 us
    convert_element_type x1, other arithmetic, shards(): mixed = mixed.astype(jnp.bfloat16)  31.3 us
    dot_general x1, matrix products, shards(): jnp.einsum('lqrc,loprc->lqop', doubled_up(coupling, 'aux', 1), sources, p...  27.3 us
  transfers between devices with their start and end apart: 5, of which 1 were waited for; matrix products, arithmetic and copies ran while one was open for 28% of the time, Pallas kernels for 0%

profile of v1, /device:TPU:20, one launch (start us, length us, event | category | flops | bytes accessed | tf_op | source)
XLA Modules:
  0.0 655.9 jit_solution(16649537972283831874)
XLA Ops:
  0.1 1.0 select_reduce_fusion.1
  1.2 5.5 all_gather.6
  7.0 1.7 collective-permute-start.2
  9.1 0.8 select_reduce_fusion.4
  9.9 0.8 select_reduce_fusion
  11.2 10.6 %broadcast_select_fusion = bf16[2,64,128,384]{3,2,1,0:T(8,128)(2,1)} fusion(bf16[2,64,128,384]{3,2,1,0:T(8,128)(2,1)} %param.7, pred[2,128,384]{2,1,0:T(8,128)(4,1)S(1)} %and_and_fusion), kind=kLoop, calls=%fused_computation.17 | loop fusion | flops 6291456 | bytes 25264128 | tf_op jit(solution)/shard_map/jit(_where)/select_n | solution.py:89
  21.7 1.5 collective-permute-start
  23.2 14.0 %fusion.17 = f32[2,64,128,384]{3,2,1,0:T(8,128)} fusion(bf16[2,128,384,1]{2,1,3,0:T(8,128)(2,1)S(1)} %bitcast.84, bf16[2,64,128,384]{3,2,1,0:T(8,128)(2,1)} %broadcast_select_fusion), kind=kOutput, calls=%fused_computation.22 | convolution fusion | flops 1610612736 | bytes 29556736 | tf_op jit(solution)/shard_map/lpmb,lbc->lpmc/dot_general | solution.py:102
  37.3 258.9 %all_gather.7 = bf16[256,384]{1,0:T(8,128)(2,1)S(1)} all-gather(bf16[128,384]{1,0:T(8,128)(2,1)S(1)} %copy-done.1), channel_id=1, replica_groups=mesh['atom'=16,'aux'=2] {'aux'}, dimensions={0}, use_global_device_ids=true | all-gather | bytes 294912 | tf_op jit(solution)/shard_map/all_gather | solution.py:91
  296.5 13.9 %fusion.15 = f32[2,64,128,384]{3,2,1,0:T(8,128)} fusion(bf16[2,128,384,1]{2,1,3,0:T(8,128)(2,1)S(1)} %bitcast.91, bf16[2,64,128,384]{3,2,1,0:T(8,128)(2,1)} %broadcast_select_fusion), kind=kOutput, calls=%fused_computation.20 | convolution fusion | flops 1610612736 | bytes 29556736 | tf_op jit(solution)/shard_map/lpmb,lbc->lpmc/dot_general | solution.py:102
  310.4 13.9 %fusion.19 = f32[2,64,128,384]{3,2,1,0:T(8,128)} fusion(bf16[2,128,384,1]{2,1,3,0:T(8,128)(2,1)S(1)} %bitcast.90, bf16[2,64,128,384]{3,2,1,0:T(8,128)(2,1)} %broadcast_select_fusion), kind=kOutput, calls=%fused_computation.24 | convolution fusion | flops 1610612736 | bytes 29556736 | tf_op jit(solution)/shard_map/lpmb,lbc->lpmc/dot_general | solution.py:102
  324.3 31.3 %add_convert_fusion = bf16[2,64,128,640]{3,2,1,0:T(8,128)(2,1)} fusion(f32[2,64,128,384]{3,2,1,0:T(8,128)} %fusion.15, f32[2,64,128,384]{3,2,1,0:T(8,128)} %fusion.17, f32[2,64,128,384]{3,2,1,0:T(8,128)} %fusion.19), kind=kLoop, calls=%fused_computation | loop fusion | flops 31457280 | bytes 96468992 | tf_op jit(solution)/shard_map/convert_element_type | solution.py:109
  355.6 10.6 %convert_bitcast_fusion.2 = bf16[2,64,128,384]{2,3,1,0:T(8,128)(2,1)} fusion(bf16[2,64,128,640]{3,2,1,0:T(8,128)(2,1)} %add_convert_fusion, bf16[2,128,384]{2,1,0:T(8,128)(2,1)S(1)} %bitcast.87), kind=kOutput, calls=%fused_computation.16 | convolution fusion | flops 1616904192 | bytes 25231360 | tf_op jit(solution)/shard_map/lmj,lpmc->lpjc/dot_general | solution.py:114
  366.2 12.5 %slice_bitcast_fusion.1 = (bf16[64,128,384]{1,2,0:T(8,128)(2,1)}, bf16[1,64,128,384]{2,3,1,0:T(8,128)(2,1)}) fusion(bf16[2,64,128,384]{2,3,1,0:T(8,128)(2,1)} %convert_bitcast_fusion.2), kind=kLoop, calls=%fused_computation.19 | loop fusion | bytes 25165824 | tf_op jit(solution)/shard_map/squeeze | solution.py:121
  378.7 10.6 %convert_bitcast_fusion = bf16[2,64,128,384]{2,3,1,0:T(8,128)(2,1)} fusion(bf16[2,64,128,640]{3,2,1,0:T(8,128)(2,1)} %add_convert_fusion, bf16[2,128,384]{2,1,0:T(8,128)(2,1)S(1)} %bitcast.88), kind=kOutput, calls=%fused_computation.14 | convolution fusion | flops 1616904192 | bytes 25231360 | tf_op jit(solution)/shard_map/lmj,lpmc->lpjc/dot_general | solution.py:114
  389.3 12.8 %fusion.26 = (bf16[1,64,128,384]{2,3,1,0:T(8,128)(2,1)}, bf16[64,128,384]{1,2,0:T(8,128)(2,1)}) fusion(bf16[2,64,128,384]{2,3,1,0:T(8,128)(2,1)} %convert_bitcast_fusion), kind=kLoop, calls=%fused_computation.60 | loop fusion | bytes 25165824 | tf_op jit(solution)/shard_map/slice | solution.py:124
  402.1 1.7 collective-permute-start.4
  403.8 10.7 %convert_bitcast_fusion.1 = bf16[2,1,64,128,384]{3,4,2,0,1:T(8,128)(2,1)} fusion(bf16[2,64,128,640]{3,2,1,0:T(8,128)(2,1)} %add_convert_fusion, bf16[2,128,384]{2,1,0:T(8,128)(2,1)S(1)} %bitcast.89), kind=kOutput, calls=%fused_computation.15 | convolution fusion | flops 1616904192 | bytes 25231360 | tf_op jit(solution)/shard_map/lmj,lpmc->lpjc/dot_general | solution.py:114
  414.5 102.4 %collective-permute-done.3 = bf16[64,128,384]{1,2,0:T(8,128)(2,1)} collective-permute-done((bf16[64,128,384]{1,2,0:T(8,128)(2,1)}, bf16[64,128,384]{1,2,0:T(8,128)(2,1)}, u32[]{:S(2)}, u32[]{:S(2)}) %collective-permute-start.3) | collective-permute-done | bytes 6291488 | tf_op jit(solution)/shard_map/ppermute | solution.py:38
  516.9 9.2 %maximum_bitcast_fusion = bf16[2,1,64,128,384]{3,4,2,0,1:T(8,128)(2,1)} fusion(bf16[1,64,128,384]{2,3,1,0:T(8,128)(2,1)S(1)} %bitcast.83, bf16[1,64,128,384]{2,3,1,0:T(8,128)(2,1)} %bitcast.16), kind=kLoop, calls=%fused_computation.12 | loop fusion | flops 6291456 | bytes 25165824 | tf_op jit(solution)/shard_map/stack | solution.py:125
  526.1 8.3 %maximum_bitcast_fusion.1 = bf16[2,1,64,128,384]{3,4,2,0,1:T(8,128)(2,1)} fusion(bf16[1,64,128,384]{2,3,1,0:T(8,128)(2,1)} %bitcast.26, bf16[1,64,128,384]{2,3,1,0:T(8,128)(2,1)S(1)} %copy-done), kind=kLoop, calls=%fused_computation.13 | loop fusion | flops 6291456 | bytes 25165824 | tf_op jit(solution)/shard_map/stack | solution.py:125
  534.4 25.7 %pad_maximum_fusion = bf16[2,3,64,128,384]{3,4,2,0,1:T(8,128)(2,1)} fusion(bf16[2,1,64,128,384]{3,4,2,0,1:T(8,128)(2,1)} %maximum_bitcast_fusion.1, bf16[2,1,64,128,384]{3,4,2,0,1:T(8,128)(2,1)} %convert_bitcast_fusion.1, bf16[2,1,64,128,384]{3,4,2,0,1:T(8,128)(2,1)} %maximum_bitcast_fusion), kind=kLoop, calls=%fused_computation.1 | loop fusion | flops 37748736 | bytes 75497472 | tf_op jit(solution)/shard_map/stack | solution.py:125
  560.1 24.8 %fusion.2 = bf16[2,128,128,384,1]{3,2,1,0,4:T(8,128)(2,1)} fusion(bf16[2,64,128,384]{3,2,1,0:T(8,128)(2,1)} %collective-permute-done, bf16[2,64,128,384]{3,2,1,0:T(8,128)(2,1)} %broadcast_select_fusion, pred[]{:T(512)S(6)} %eq.22), kind=kLoop, calls=%fused_computation.5 | loop fusion | flops 37748736 | bytes 50331648 | tf_op jit(solution)/shard_map/jit(_where)/select_n | solution.py:14
  584.9 32.2 %copy.65 = bf16[2,128,128,384,1]{2,1,3,4,0:T(8,128)(2,1)} copy(bf16[2,128,128,384,1]{3,2,1,0,4:T(8,128)(2,1)} %fusion.2) | data formatting | bytes 50331648 | tf_op jit(solution)/shard_map/jit(_where)/select_n | solution.py:14
  617.1 27.3 %fusion.21 = f32[2,128,3,64]{1,3,2,0:T(8,128)S(1)} fusion(bf16[2,128,128,384,1]{2,1,3,4,0:T(8,128)(2,1)} %copy.65, bf16[2,3,64,128,384]{3,4,2,0,1:T(8,128)(2,1)} %pad_maximum_fusion), kind=kOutput, calls=%fused_computation.26 | convolution fusion | flops 4831838208 | bytes 63111168 | tf_op jit(solution)/shard_map/lqrc,loprc->lqop/dot_general | solution.py:127
  644.7 0.4 reshape.145
  645.1 7.4 %all_to_all.15 = f32[2,1,24576]{2,1,0:T(1,128)S(1)} all-to-all(f32[2,1,24576]{2,1,0:T(1,128)S(1)} %reshape.145), channel_id=1, replica_groups=mesh['atom'=16,'aux'=2] {'aux'}, dimensions={0} | all-to-all | bytes 393216 | tf_op jit(solution)/shard_map/all_to_all | solution.py:133
  652.5 0.5 broadcast.157
  653.0 1.2 reduce
  654.2 0.4 reshape.146
  654.6 0.3 copy.55
  654.9 1.0 reshape.136
  (40 shorter events, 1.9 us)
Async XLA Ops:
  6.9 289.5 %collective-permute-start.1 = (bf16[128,384]{1,0:T(8,128)(2,1)S(1)}, bf16[128,384]{1,0:T(8,128)(2,1)S(1)}, u32[]{:S(2)}, u32[]{:S(2)}) collective-permute-start(bf16[128,384]{1,0:T(8,128)(2,1)S(1)} %get-tuple-element.14), channel_id=1, source_target_pairs={{0,2},{2,4},{4,6},{6,8},{8,10},{10,12},{12,14},{14,16},{16,18},{18... | collective-permute-start | bytes 294920 | tf_op jit(solution)/shard_map/ppermute | solution.py:26
  7.0 289.4 %collective-permute-start.2 = (bf16[128,384]{1,0:T(8,128)(2,1)S(1)}, bf16[128,384]{1,0:T(8,128)(2,1)S(1)}, u32[]{:S(2)}, u32[]{:S(2)}) collective-permute-start(bf16[128,384]{1,0:T(8,128)(2,1)S(1)} %get-tuple-element.15), channel_id=1, source_target_pairs={{2,0},{4,2},{6,4},{8,6},{10,8},{12,10},{14,12},{16,14},{18,16},{20... | collective-permute-start | bytes 294920 | tf_op jit(solution)/shard_map/ppermute | solution.py:28
  21.7 538.3 %collective-permute-start = (bf16[2,64,128,384]{3,2,1,0:T(8,128)(2,1)}, bf16[2,64,128,384]{3,2,1,0:T(8,128)(2,1)}, u32[]{:S(2)}, u32[]{:S(2)}) collective-permute-start(bf16[2,64,128,384]{3,2,1,0:T(8,128)(2,1)} %broadcast_select_fusion), channel_id=1, source_target_pairs={{0,1},{1,0},{2,3},{3,2},{4,5},{5,4},{6,7},{7,6},{8,9},{9,8},{10,11... | collective-permute-start | bytes 37748744 | tf_op jit(solution)/shard_map/ppermute | solution.py:11
  23.2 14.1 %copy-start.1 = (bf16[128,384]{1,0:T(8,128)(2,1)S(1)}, bf16[128,384]{1,0:T(8,128)(2,1)}, u32[]{:S(2)}) copy-start(bf16[128,384]{1,0:T(8,128)(2,1)} %param.8) | copy-start | bytes 294916
  378.7 138.1 %collective-permute-start.3 = (bf16[64,128,384]{1,2,0:T(8,128)(2,1)}, bf16[64,128,384]{1,2,0:T(8,128)(2,1)}, u32[]{:S(2)}, u32[]{:S(2)}) collective-permute-start(bf16[64,128,384]{1,2,0:T(8,128)(2,1)} %get-tuple-element.8), channel_id=1, source_target_pairs={{0,2},{2,4},{4,6},{6,8},{8,10},{10,12},{12,14},{14,16},{16,18},{18... | collective-permute-start | bytes 18874376 | tf_op jit(solution)/shard_map/ppermute | solution.py:38
  389.3 127.5 %slice-start = ((s8[6291456]{0:T(1024)(128)(4,1)}), s8[2097152]{0:T(1024)(128)(4,1)S(1)}, s32[]{:S(2)}) async-start(s8[6291456]{0:T(1024)(128)(4,1)} %bitcast.82), calls=%async_computation.1 | async-start | bytes 4194304
  402.1 124.0 %collective-permute-start.4 = (bf16[64,128,384]{1,2,0:T(8,128)(2,1)}, bf16[64,128,384]{1,2,0:T(8,128)(2,1)}, u32[]{:S(2)}, u32[]{:S(2)}) collective-permute-start(bf16[64,128,384]{1,2,0:T(8,128)(2,1)} %get-tuple-element.11), channel_id=1, source_target_pairs={{0,30},{2,0},{4,2},{6,4},{8,6},{10,8},{12,10},{14,12},{16,14},{18,... | collective-permute-start | bytes 18874376 | tf_op jit(solution)/shard_map/ppermute | solution.py:38
  403.8 113.0 %slice-start.1 = ((s8[6291456]{0:T(1024)(128)(4,1)}), s8[4194304]{0:T(1024)(128)(4,1)S(1)}, s32[]{:S(2)}) async-start(s8[6291456]{0:T(1024)(128)(4,1)} %bitcast.82), calls=%async_computation.2 | async-start | bytes 8388608
  516.8 9.2 %copy-start = (bf16[1,64,128,384]{2,3,1,0:T(8,128)(2,1)S(1)}, bf16[1,64,128,384]{2,3,1,0:T(8,128)(2,1)}, u32[]{:S(2)}) copy-start(bf16[1,64,128,384]{2,3,1,0:T(8,128)(2,1)} %get-tuple-element.10) | copy-start | bytes 18874372
